TPU v7x, 512 devices: a whole 4x8x8 slice. The times are simulated.
512 devices in a mesh: cfg: 2 (over z_lo), section: 8 (over z_hi, core), patch: 32 (over x, y).
Axes of the slice: x: 4, y: 8, z: 8 (z_hi: 4, z_lo: 2; z = z_hi * 2 + z_lo), core: 2. Of those that a mesh axis runs over, the one named last changes fastest.
Arguments:
- inputs: bfloat16 [2, 1024, 1536], P('cfg', 'patch'), may hold values from -6 to 6
- stale_kv: bfloat16 [2, 8, 2, 1024, 1536], P('cfg', 'section', None, 'patch'), may hold values from -6 to 6
- q_gain: float32 [8, 1536], P('section'), may hold values from 0.3 to 1.2
- k_gain: float32 [8, 1536], P('section'), may hold values from 0.3 to 1.2
- v_gain: float32 [8, 1536], P('section'), may hold values from 0.5 to 2
- o_gain: float32 [8, 1536], P('section'), may hold values from 2 to 8
Outputs:
- guided: bfloat16 [1024, 1536], P('patch', ('cfg', 'section'))
- fresh_kv: bfloat16 [2, 8, 2, 1024, 1536], P('cfg', 'section', None, 'patch')
All inputs are finite; a program needn't handle non-finite values.
Results may differ from a plain program's by a relative error of at most 0.017.
Values may be sent and summed in bfloat16 or wider, within the bound.
A program may use at most 64 MiB of HBM per device.

v0:
```python
import jax
import jax.numpy as jnp
from jax import lax
from jax.sharding import PartitionSpec as P

HEADS = 12
HD = 128
MB = 8


guide_scale = 6.0


def shifted(value, axis, by):
    length = lax.axis_size(axis)
    pairs = [(i, i + by) for i in range(length) if 0 <= i + by < length]
    return lax.ppermute(value, axis, pairs)


def partner_2(block, axis, bit):
    count = lax.axis_size(axis)
    route = []
    for low in range(count):
        high = low | 1 << bit
        if high != low and high < count:
            route += [(low, high), (high, low)]
    return lax.ppermute(block, axis, route)


def broadcast(value, axis, root):
    mine = lax.axis_index(axis) == root
    return lax.psum(jnp.where(mine, value, jnp.zeros_like(value)), axis)


def prepare(block, q_row, k_row, v_row):
    rows = block.shape[0]
    wide = block.astype(jnp.float32)
    split = wide.reshape(rows, HEADS, HD)
    normed = split * lax.rsqrt(jnp.mean(split * split, axis=2, keepdims=True) + 1e-06)
    normed = normed.reshape(rows, HEADS * HD)
    query = (normed * q_row).astype(jnp.bfloat16)
    key = (normed * k_row).astype(jnp.bfloat16)
    value = (wide * v_row).astype(jnp.bfloat16)
    return (query, key, value)


def attend_split(query, far_keys, far_vals, near_keys, near_vals, own_start):
    rows = query.shape[0]
    count = far_keys.shape[0]
    near_count = near_keys.shape[0]
    q_heads = query.reshape(rows, HEADS, HD)
    scale = HD ** (-0.5)
    far_scores = (
        jnp.einsum(
            "rhd,nhd->hrn",
            q_heads,
            far_keys.reshape(count, HEADS, HD),
            preferred_element_type=jnp.float32,
        )
        * scale
    )
    near_scores = (
        jnp.einsum(
            "rhd,nhd->hrn",
            q_heads,
            near_keys.reshape(near_count, HEADS, HD),
            preferred_element_type=jnp.float32,
        )
        * scale
    )
    columns = lax.iota(jnp.int32, count)
    inside = (columns >= own_start) & (columns < own_start + near_count)
    far_scores = jnp.where(inside[None, None, :], -1e30, far_scores)
    top = jnp.maximum(
        jnp.max(far_scores, axis=2, keepdims=True), jnp.max(near_scores, axis=2, keepdims=True)
    )
    far_exp = jnp.exp(far_scores - top)
    near_exp = jnp.exp(near_scores - top)
    total = jnp.sum(far_exp, axis=2, keepdims=True) + jnp.sum(near_exp, axis=2, keepdims=True)
    far_weights = (far_exp / total).astype(jnp.bfloat16)
    near_weights = (near_exp / total).astype(jnp.bfloat16)
    mixed = jnp.einsum(
        "hrn,nhd->rhd",
        far_weights,
        far_vals.reshape(count, HEADS, HD),
        preferred_element_type=jnp.float32,
    )
    mixed = mixed + jnp.einsum(
        "hrn,nhd->rhd",
        near_weights,
        near_vals.reshape(near_count, HEADS, HD),
        preferred_element_type=jnp.float32,
    )
    return mixed.reshape(rows, HEADS * HD)


def local(inputs, stale_kv, q_gain, k_gain, v_gain, o_gain):
    tok = inputs.shape[1]
    width = inputs.shape[2]
    blk = tok // MB
    sections = lax.axis_size("section")
    section_at = lax.axis_index("section")
    patch_at = lax.axis_index("patch")
    own_kv = stale_kv[0, 0]
    gathered = lax.all_gather(own_kv, "patch", axis=1, tiled=True)
    own_start = patch_at * tok
    buffer = own_kv
    held = jnp.zeros((blk, width), jnp.bfloat16)
    final = jnp.zeros((tok, width), jnp.bfloat16)
    turns = MB + sections - 1
    for turn in range(turns):
        micro = turn - section_at
        valid = (micro >= 0) & (micro < MB)
        start = jnp.clip(micro, 0, MB - 1) * blk
        first = lax.dynamic_slice_in_dim(inputs[0], start, blk, 0)
        block = jnp.where(section_at == 0, first, held)
        query, key, value = prepare(block, q_gain[0], k_gain[0], v_gain[0])
        fresh = jnp.stack([key, value])
        updated = lax.dynamic_update_slice_in_dim(buffer, fresh, start, 1)
        buffer = jnp.where(valid, updated, buffer)
        current = buffer
        mixed = lax.cond(
            valid,
            lambda: attend_split(
                query, gathered[0], gathered[1], current[0], current[1], own_start
            ),
            lambda: jnp.zeros((blk, width), jnp.float32),
        )
        result = (block.astype(jnp.float32) + o_gain[0] * mixed).astype(jnp.bfloat16)
        placed = lax.dynamic_update_slice_in_dim(final, result, start, 0)
        final = jnp.where(valid & (section_at == sections - 1), placed, final)
        if turn + 1 < turns:
            held = shifted(result, "section", 1)
    branch = lax.axis_index("cfg")
    partner = partner_2(final, "cfg", 0)
    uncond = jnp.where(branch == 0, final, partner).astype(jnp.float32)
    cond = jnp.where(branch == 0, partner, final).astype(jnp.float32)
    guided = uncond + guide_scale * (cond - uncond)
    guided = guided.astype(jnp.bfloat16)
    half_width = width // 2
    part_width = half_width // sections
    guided = broadcast(guided, "section", sections - 1)
    guided = lax.dynamic_slice_in_dim(
        guided, (branch * sections + section_at) * part_width, part_width, 1
    )
    return (guided, buffer[None, None])


def solution(mesh):
    placed = (
        P("cfg", "patch", None),
        P("cfg", "section", None, "patch", None),
        P("section", None),
        P("section", None),
        P("section", None),
        P("section", None),
    )
    return jax.shard_map(
        local,
        mesh=mesh,
        in_specs=placed,
        out_specs=(P("patch", ("cfg", "section")), P("cfg", "section", None, "patch", None)),
        check_vma=False,
    )
```

profile of v0, /device:TPU:1, one launch (start us, length us, event | category | flops | bytes accessed | tf_op | source)
XLA Modules:
  0.0 784.5 jit_solution(9921352858136029199)
XLA Ops:
  7.2 1.8 copy.219
  17.6 92.3 %all-gather.3.cloned.1.call-done = bf16[1,1,2,1024,1536]{4,2,1,0,3:T(2,128)(2,1)} async-done(((bf16[1,1,2,32,1536]{4,2,1,0,3:T(2,128)(2,1)}), bf16[1,1,2,1024,1536]{4,2,1,0,3:T(2,128)(2,1)}) %all-gather.3.cloned.1.call-update) | async-done | bytes 6291472 | tf_op jit(solution)/shard_map/all_gather | solution.py:105
  110.7 5.6 collective-permute-start
  116.3 26.1 %collective-permute-done = bf16[4,1536]{1,0:T(4,128)(2,1)S(1)} collective-permute-done((bf16[4,1536]{1,0:T(4,128)(2,1)S(1)}, bf16[4,1536]{1,0:T(4,128)(2,1)S(1)}, u32[]{:S(2)}, u32[]{:S(2)}) %collective-permute-start) | collective-permute-done | bytes 12320 | tf_op jit(solution)/shard_map/ppermute | solution.py:17
  144.8 32.2 %conditional.16 = (f32[4,1536]{1,0:T(4,128)S(1)}) conditional(s32[]{:T(128)} %convert_element_type.409, () %tuple.100, (s32[]{:T(128)}, bf16[4,1536]{1,0:T(4,128)(2,1)S(1)}, bf16[2,1024,1536]{2,0,1:T(2,128)(2,1)}, bf16[2,32,1536]{2,1,0:T(8,128)(2,1)}) %tuple.282), branch_computations={%region_8.9_spmd, %region_9.14_spmd} | conditional | flops 26365344 | bytes 33152028 | solution.py:122
  144.8 16.1 %copy.221 = bf16[2,1024,1536]{1,2,0:T(8,128)(2,1)} copy(bf16[2,1024,1536]{2,0,1:T(2,128)(2,1)} %get-tuple-element.233) | data formatting | bytes 12582912 | tf_op jit(solution)/shard_map
  161.0 5.2 fusion.367
  166.2 2.5 fusion.369
  168.7 1.6 fusion.368
  177.0 1.9 collective-permute-start.1
  182.6 32.2 %conditional.17 = (f32[4,1536]{1,0:T(4,128)S(1)}) conditional(s32[]{:T(128)} %convert_element_type.415, () %tuple.102, (s32[]{:T(128)}, bf16[4,1536]{1,0:T(4,128)(2,1)S(1)}, bf16[2,1024,1536]{2,0,1:T(2,128)(2,1)}, bf16[2,32,1536]{2,1,0:T(8,128)(2,1)}) %tuple.283), branch_computations={%region_15.16_spmd, %region_16.21_spmd} | conditional | flops 26365344 | bytes 33152028 | solution.py:122
  182.6 16.1 %copy.222 = bf16[2,1024,1536]{1,2,0:T(8,128)(2,1)} copy(bf16[2,1024,1536]{2,0,1:T(2,128)(2,1)} %get-tuple-element.237) | data formatting | bytes 12582912 | tf_op jit(solution)/shard_map
  198.7 5.2 fusion.371
  203.9 2.5 fusion.373
  206.4 1.6 fusion.372
  214.8 4.8 collective-permute-start.2
  222.8 32.6 %conditional.18 = (f32[4,1536]{1,0:T(4,128)S(1)}) conditional(s32[]{:T(128)} %convert_element_type.421, () %tuple.104, (s32[]{:T(128)}, bf16[4,1536]{1,0:T(4,128)(2,1)S(1)}, bf16[2,1024,1536]{2,0,1:T(2,128)(2,1)}, bf16[2,32,1536]{2,1,0:T(8,128)(2,1)}) %tuple.284), branch_computations={%region_22.23_spmd, %region_23.28_spmd} | conditional | flops 26365344 | bytes 33152028 | solution.py:122
  223.2 16.2 %copy.223 = bf16[2,1024,1536]{1,2,0:T(8,128)(2,1)} copy(bf16[2,1024,1536]{2,0,1:T(2,128)(2,1)} %get-tuple-element.241) | data formatting | bytes 12582912 | tf_op jit(solution)/shard_map
  239.4 5.2 fusion.375
  244.6 2.5 fusion.377
  247.1 1.6 fusion.376
  248.7 1.6 squeeze.130
  255.5 5.1 collective-permute-start.3
  263.8 32.2 %conditional.19 = (f32[4,1536]{1,0:T(4,128)S(1)}) conditional(s32[]{:T(128)} %convert_element_type.427, () %tuple.106, (s32[]{:T(128)}, bf16[4,1536]{1,0:T(4,128)(2,1)S(1)}, bf16[2,1024,1536]{2,0,1:T(2,128)(2,1)}, bf16[2,32,1536]{2,1,0:T(8,128)(2,1)}) %tuple.285), branch_computations={%region_29.30_spmd, %region_30.35_spmd} | conditional | flops 26365344 | bytes 33152028 | solution.py:122
  263.8 16.1 %copy.224 = bf16[2,1024,1536]{1,2,0:T(8,128)(2,1)} copy(bf16[2,1024,1536]{2,0,1:T(2,128)(2,1)} %get-tuple-element.245) | data formatting | bytes 12582912 | tf_op jit(solution)/shard_map
  280.0 5.2 fusion.379
  285.2 2.5 fusion.381
  287.7 1.6 fusion.380
  296.0 5.1 collective-permute-start.4
  304.4 32.2 %conditional.20 = (f32[4,1536]{1,0:T(4,128)S(1)}) conditional(s32[]{:T(128)} %convert_element_type.433, () %tuple.108, (s32[]{:T(128)}, bf16[4,1536]{1,0:T(4,128)(2,1)S(1)}, bf16[2,1024,1536]{2,0,1:T(2,128)(2,1)}, bf16[2,32,1536]{2,1,0:T(8,128)(2,1)}) %tuple.286), branch_computations={%region_36.37_spmd, %region_37.42_spmd} | conditional | flops 26365344 | bytes 33152028 | solution.py:122
  304.4 16.1 %copy.225 = bf16[2,1024,1536]{1,2,0:T(8,128)(2,1)} copy(bf16[2,1024,1536]{2,0,1:T(2,128)(2,1)} %get-tuple-element.249) | data formatting | bytes 12582912 | tf_op jit(solution)/shard_map
  320.5 5.2 fusion.383
  325.8 2.5 fusion.385
  328.3 1.6 fusion.384
  329.9 1.6 squeeze.158
  336.6 5.1 collective-permute-start.5
  345.0 32.2 %conditional.21 = (f32[4,1536]{1,0:T(4,128)S(1)}) conditional(s32[]{:T(128)} %convert_element_type.439, () %tuple.110, (s32[]{:T(128)}, bf16[4,1536]{1,0:T(4,128)(2,1)S(1)}, bf16[2,1024,1536]{2,0,1:T(2,128)(2,1)}, bf16[2,32,1536]{2,1,0:T(8,128)(2,1)}) %tuple.287), branch_computations={%region_43.44_spmd, %region_44.49_spmd} | conditional | flops 26365344 | bytes 33152028 | solution.py:122
  345.0 16.1 %copy.226 = bf16[2,1024,1536]{1,2,0:T(8,128)(2,1)} copy(bf16[2,1024,1536]{2,0,1:T(2,128)(2,1)} %get-tuple-element.253) | data formatting | bytes 12582912 | tf_op jit(solution)/shard_map
  361.1 5.2 fusion.387
  366.3 2.5 fusion.389
  368.8 1.6 fusion.388
  370.4 1.6 squeeze.162
  377.2 5.3 collective-permute-start.6
  385.5 32.2 %conditional.22 = (f32[4,1536]{1,0:T(4,128)S(1)}) conditional(s32[]{:T(128)} %convert_element_type.445, () %tuple.112, (s32[]{:T(128)}, bf16[4,1536]{1,0:T(4,128)(2,1)S(1)}, bf16[2,1024,1536]{2,0,1:T(2,128)(2,1)}, bf16[2,32,1536]{2,1,0:T(8,128)(2,1)}) %tuple.288), branch_computations={%region_50.51_spmd, %region_51.56_spmd} | conditional | flops 26365344 | bytes 33152028 | solution.py:122
  385.5 16.1 %copy.227 = bf16[2,1024,1536]{1,2,0:T(8,128)(2,1)} copy(bf16[2,1024,1536]{2,0,1:T(2,128)(2,1)} %get-tuple-element.257) | data formatting | bytes 12582912 | tf_op jit(solution)/shard_map
  401.7 5.2 fusion.391
  406.9 2.5 fusion.393
  409.4 1.6 fusion.392
  417.7 5.1 collective-permute-start.7
  426.1 32.2 %conditional.23 = (f32[4,1536]{1,0:T(4,128)S(1)}) conditional(s32[]{:T(128)} %convert_element_type.451, () %tuple.114, (s32[]{:T(128)}, bf16[4,1536]{1,0:T(4,128)(2,1)S(1)}, bf16[2,1024,1536]{2,0,1:T(2,128)(2,1)}, bf16[2,32,1536]{2,1,0:T(8,128)(2,1)}) %tuple.289), branch_computations={%region_57.58_spmd, %region_58.63_spmd} | conditional | flops 26365344 | bytes 33152028 | solution.py:122
  426.1 16.1 %copy.228 = bf16[2,1024,1536]{1,2,0:T(8,128)(2,1)} copy(bf16[2,1024,1536]{2,0,1:T(2,128)(2,1)} %get-tuple-element.261) | data formatting | bytes 12582912 | tf_op jit(solution)/shard_map
  442.2 5.2 fusion.395
  447.5 2.5 fusion.397
  450.0 1.6 fusion.396
  451.6 1.6 squeeze.170
  458.3 5.1 collective-permute-start.8
  466.7 37.3 %collective-permute-start.9 = (bf16[4,1536]{1,0:T(4,128)(2,1)S(1)}, bf16[4,1536]{1,0:T(4,128)(2,1)S(1)}, u32[]{:S(2)}, u32[]{:S(2)}) collective-permute-start(bf16[4,1536]{1,0:T(4,128)(2,1)S(1)} %get-tuple-element.306), channel_id=1, source_target_pairs={{0,32},{32,64},{64,96},{96,128},{128,160},{160,192},{192,224},{1,3... | collective-permute-start | bytes 36872 | tf_op jit(solution)/shard_map/ppermute | solution.py:17
  507.3 5.3 collective-permute-start.10
  515.7 35.3 %collective-permute-start.11 = (bf16[4,1536]{1,0:T(4,128)(2,1)S(1)}, bf16[4,1536]{1,0:T(4,128)(2,1)S(1)}, u32[]{:S(2)}, u32[]{:S(2)}) collective-permute-start(bf16[4,1536]{1,0:T(4,128)(2,1)S(1)} %get-tuple-element.298), channel_id=1, source_target_pairs={{0,32},{32,64},{64,96},{96,128},{128,160},{160,192},{192,224},{1,3... | collective-permute-start | bytes 36872 | tf_op jit(solution)/shard_map/ppermute | solution.py:17
  554.3 6.3 collective-permute-start.12
  563.9 38.5 %collective-permute-start.13 = (bf16[4,1536]{1,0:T(4,128)(2,1)S(1)}, bf16[4,1536]{1,0:T(4,128)(2,1)S(1)}, u32[]{:S(2)}, u32[]{:S(2)}) collective-permute-start(bf16[4,1536]{1,0:T(4,128)(2,1)S(1)} %get-tuple-element.290), channel_id=1, source_target_pairs={{0,32},{32,64},{64,96},{96,128},{128,160},{160,192},{192,224},{1,3... | collective-permute-start | bytes 36872 | tf_op jit(solution)/shard_map/ppermute | solution.py:17
  605.7 3.3 collective-permute-start.14
  609.0 2.1 collective-permute-done.14
  611.8 164.2 %all-reduce.2.cloned.1.call-done = bf16[32,1536]{1,0:T(8,128)(2,1)} async-done(((bf16[32,1536]{1,0:T(8,128)(2,1)}), bf16[32,1536]{1,0:T(8,128)(2,1)}) %all-reduce.2.cloned.1.call-update) | async-done | bytes 98320 | tf_op jit(solution)/shard_map/psum | solution.py:32
  (252 shorter events, 103.0 us)
Async XLA Ops:
  7.2 102.7 %all-gather.3.cloned.1.call-start = ((), (), s32[]{:S(2)}) async-start(), calls=%async_computation.1 | async-start | bytes 6488064 | tf_op jit(solution)/shard_map/all_gather | solution.py:105
  9.0 767.0 %all-reduce.2.cloned.1.call-start = ((), (), s32[]{:S(2)}) async-start(), calls=%async_computation | async-start | bytes 196608 | tf_op jit(solution)/shard_map/psum | solution.py:32
  110.7 31.7 %collective-permute-start = (bf16[4,1536]{1,0:T(4,128)(2,1)S(1)}, bf16[4,1536]{1,0:T(4,128)(2,1)S(1)}, u32[]{:S(2)}, u32[]{:S(2)}) collective-permute-start(bf16[4,1536]{1,0:T(4,128)(2,1)S(1)} %get-tuple-element.342), channel_id=1, source_target_pairs={{0,32},{32,64},{64,96},{96,128},{128,160},{160,192},{192,224},{1,3... | collective-permute-start | bytes 36872 | tf_op jit(solution)/shard_map/ppermute | solution.py:17
  177.0 3.1 collective-permute-start.1
  214.8 5.6 collective-permute-start.2
  255.5 5.9 collective-permute-start.3
  296.0 5.9 collective-permute-start.4
  336.6 5.9 collective-permute-start.5
  377.2 5.9 collective-permute-start.6
  417.7 5.9 collective-permute-start.7
  458.3 5.9 collective-permute-start.8
  466.7 38.1 %collective-permute-start.9 = (bf16[4,1536]{1,0:T(4,128)(2,1)S(1)}, bf16[4,1536]{1,0:T(4,128)(2,1)S(1)}, u32[]{:S(2)}, u32[]{:S(2)}) collective-permute-start(bf16[4,1536]{1,0:T(4,128)(2,1)S(1)} %get-tuple-element.306), channel_id=1, source_target_pairs={{0,32},{32,64},{64,96},{96,128},{128,160},{160,192},{192,224},{1,3... | collective-permute-start | bytes 36872 | tf_op jit(solution)/shard_map/ppermute | solution.py:17
  507.3 5.9 collective-permute-start.10
  515.7 36.2 %collective-permute-start.11 = (bf16[4,1536]{1,0:T(4,128)(2,1)S(1)}, bf16[4,1536]{1,0:T(4,128)(2,1)S(1)}, u32[]{:S(2)}, u32[]{:S(2)}) collective-permute-start(bf16[4,1536]{1,0:T(4,128)(2,1)S(1)} %get-tuple-element.298), channel_id=1, source_target_pairs={{0,32},{32,64},{64,96},{96,128},{128,160},{160,192},{192,224},{1,3... | collective-permute-start | bytes 36872 | tf_op jit(solution)/shard_map/ppermute | solution.py:17
  554.3 7.1 collective-permute-start.12
  563.9 39.3 %collective-permute-start.13 = (bf16[4,1536]{1,0:T(4,128)(2,1)S(1)}, bf16[4,1536]{1,0:T(4,128)(2,1)S(1)}, u32[]{:S(2)}, u32[]{:S(2)}) collective-permute-start(bf16[4,1536]{1,0:T(4,128)(2,1)S(1)} %get-tuple-element.290), channel_id=1, source_target_pairs={{0,32},{32,64},{64,96},{96,128},{128,160},{160,192},{192,224},{1,3... | collective-permute-start | bytes 36872 | tf_op jit(solution)/shard_map/ppermute | solution.py:17
  605.7 5.4 collective-permute-start.14
Sparse Core Ops, SparseCore 0:
  11.2 98.6 all-gather.2
  611.9 164.0 all-reduce.1
where the time goes:
time: 799 us; the launch traced here: 784 us
  waiting for transfers between devices  295 us (37%)
  local copies, waits for them, and re-layouts  211 us (26%)
  starting transfers between devices  169 us (21%)
  matrix products  49.1 us (6%)
  other arithmetic  44.6 us (6%)
  between operations  15.1 us (2%)
    ppermute x14, starting transfers between devices, shifted(): return lax.ppermute(value, axis, pairs)  166 us
    psum x1, waiting for transfers between devices, broadcast(): return lax.psum(jnp.where(mine, value, jnp.zeros_like(value)), axis)  164 us
    another operation x16, local copies, waits for them, and re-layouts  129 us
    all_gather x1, waiting for transfers between devices, local(): gathered = lax.all_gather(own_kv, 'patch', axis=1, tiled=True)  92.3 us
    slice x8, local copies, waits for them, and re-layouts, local(): gathered[0]  41.8 us
    ppermute x14, waiting for transfers between devices, shifted(): return lax.ppermute(value, axis, pairs)  36.4 us
    select_n x15, other arithmetic, local(): buffer = jnp.where(valid, updated, buffer)  21.6 us
    dot_general x8, matrix products, attend_split(): jnp.einsum('rhd,nhd->hrn', q_heads, far_keys.reshape(count, HEADS, HD), p...  19.9 us
  transfers between devices with their start and end apart: 17, of which 17 were waited for; matrix products, arithmetic and copies ran while one was open for 1% of the time, Pallas kernels for 0%

commit v1 on v0

v1 whole, which is shorter than its diff:
```python
import functools
import math

import jax
import jax.numpy as jnp
from jax import lax
from jax.experimental import pallas as pl
from jax.experimental.pallas import tpu as pltpu
from jax.sharding import PartitionSpec as P

MESH = pl.DeviceIdType.MESH
HD = 128
MB = 8
PARTS = 2
CHUNKS = 2
SHIFT = 24.0
EPS = 1e-6
guide_scale = 6.0


def dot_nt(a, b):
    return lax.dot_general(a, b, (((1,), (1,)), ((), ())), preferred_element_type=jnp.float32)


def dot_nn(a, b):
    return lax.dot_general(a, b, (((1,), (0,)), ((), ())), preferred_element_type=jnp.float32)


def tiles(start, size):
    return pl.ds(pl.multiple_of(start, size), size)


def flow(
    dims, x_ref, kv_ref, qg, kg, vg, og, fs_ref, fin_ref,
    kvb, xin, xmid, xout, gb, mask,
    kv_send, x_send, g_send, nxt_send, ret_send, fin_send,
    kv_sem, xin_sem, g_sem, fs_sem, fin_sem,
):
    heads, n_sec, n_patch, tok, width, nd, slots = dims
    half = n_patch // PARTS
    rows = xin.shape[1]
    per_chunk = rows // tok
    n_tok = n_patch * tok
    blocks = n_tok // rows
    last = n_sec // 2 - 1
    out_w = width // (2 * n_sec)
    c, s, p = lax.axis_index("cfg"), lax.axis_index("section"), lax.axis_index("patch")
    zh = s // 2
    core = lax.rem(s, 2)
    s0 = zh * 2
    part = p // half
    local = lax.rem(p, half)
    head = local - local // 4
    has_unit = (lax.rem(local, 4) != 3) & (head < heads)
    is_unit = has_unit & (core == 0)
    unit_part = PARTS - 1 - part
    col = c * n_sec + s
    h_first = (out_w * col) // HD
    h_last = (out_w * col + out_w - 1) // HD
    as_int = lambda flag: flag.astype(jnp.int32)

    def owner(h, r):
        return (PARTS - 1 - r) * half + h + h // 3

    gains = (qg, kg, vg, og)

    bar = pltpu.get_barrier_semaphore()

    def hello(dev):
        pl.semaphore_signal(bar, inc=1, device_id=dev, device_id_type=MESH)

    @pl.when(is_unit)
    def _():
        for i, g in enumerate(gains):
            pltpu.make_async_copy(g.at[:, tiles(head * HD, HD)], gb.at[0, i], g_sem.at[0]).start()

        def greet(i, _):
            q = lax.rem(p + i, n_patch)

            @pl.when(i > 0)
            def _():
                hello((c, s0, q))

            hello((c, s0 + 1, q))
            return 0

        lax.fori_loop(0, n_patch, greet, 0)

        @pl.when(zh > 0)
        def _():
            hello((c, s0 - 2, p))

    def greet_units(h, _):
        hello((c, s0, owner(h, part)))
        return 0

    lax.fori_loop(0, heads, greet_units, 0)
    for branch in range(2):
        hello((branch, n_sec - 2, owner(h_first, part)))

        @pl.when(h_last > h_first)
        def _():
            hello((branch, n_sec - 2, owner(h_last, part)))

    inner = 2 * half + as_int(zh < last) + as_int(zh == last) * (half * nd)
    pl.semaphore_wait(bar, PARTS * heads + as_int(is_unit) * (inner - 1))

    def g_copy(i):
        return pltpu.make_async_remote_copy(
            src_ref=gains[i].at[:, tiles(head * HD, HD)],
            dst_ref=gb.at[1, i],
            send_sem=g_send.at[i],
            recv_sem=g_sem.at[1],
            device_id=(c, s0, p),
            device_id_type=MESH,
        )

    def x_copy(i):
        h = lax.rem(p + i, heads)
        at = lax.rem(p, half)
        return pltpu.make_async_remote_copy(
            src_ref=x_ref.at[:, tiles(h * HD, HD)],
            dst_ref=xin.at[at // per_chunk, tiles(lax.rem(at, per_chunk) * tok, tok)],
            send_sem=x_send.at[i],
            recv_sem=xin_sem.at[at // per_chunk],
            device_id=(c, 0, owner(h, part)),
            device_id_type=MESH,
        )

    def kv_copy(i):
        k = lax.rem(p + i, PARTS * heads)
        h = lax.rem(k, heads)
        to = owner(h, k // heads)
        src = kv_ref.at[:, :, tiles(h * HD, HD)]
        dst = kvb.at[core, :, tiles(p * tok, tok)]
        mine = (to == p) & (core == 0)
        far = pltpu.make_async_remote_copy(
            src_ref=src,
            dst_ref=dst,
            send_sem=kv_send.at[i],
            recv_sem=kv_sem.at[core],
            device_id=(c, s0, to),
            device_id_type=MESH,
        )
        return mine, src, dst, far

    def x_start(i, _):
        x_copy(i).start()
        return 0

    def kv_start(i, _):
        mine, src, dst, far = kv_copy(i)

        @pl.when(mine)
        def _():
            pltpu.make_async_copy(src, dst, kv_sem.at[0]).start()

        @pl.when(jnp.logical_not(mine))
        def _():
            far.start()

        return 0

    @pl.when(has_unit & (core == 1))
    def _():
        for i in range(4):
            g_copy(i).start()

    @pl.when(s == 0)
    def _():
        lax.fori_loop(0, heads, x_start, 0)

    lax.fori_loop(0, PARTS * heads, kv_start, 0)

    def next_copy(ch):
        return pltpu.make_async_remote_copy(
            src_ref=xout.at[ch],
            dst_ref=xin.at[ch],
            send_sem=nxt_send.at[ch],
            recv_sem=xin_sem.at[ch],
            device_id=(c, s0 + 2, p),
            device_id_type=MESH,
        )

    def ret_copy(ch, sec, i):
        src = (xin, xmid)[sec]
        return pltpu.make_async_remote_copy(
            src_ref=src.at[ch, tiles(i * tok, tok)],
            dst_ref=fs_ref.at[:, tiles(head * HD, HD)],
            send_sem=ret_send.at[ch, sec, i],
            recv_sem=fs_sem,
            device_id=(c, s0 + sec, unit_part * half + ch * per_chunk + i),
            device_id_type=MESH,
        )

    def fin_copy(ch, i, n):
        j = (HD * head) // out_w + n
        slot = head - (out_w * j) // HD
        return pltpu.make_async_remote_copy(
            src_ref=xout.at[ch, tiles(i * tok, tok)],
            dst_ref=fin_ref.at[slot, c],
            send_sem=fin_send.at[ch, i, n],
            recv_sem=fin_sem.at[slot],
            device_id=(j // n_sec, lax.rem(j, n_sec), unit_part * half + ch * per_chunk + i),
            device_id_type=MESH,
        )

    def attend(ch, sec, x):
        row = lambda i: gb[sec, i]
        wide = x.astype(jnp.float32)
        normed = wide * lax.rsqrt(jnp.mean(wide * wide, axis=1, keepdims=True) + EPS)
        query = (normed * row(0)).astype(jnp.bfloat16)
        key = (normed * row(1)).astype(jnp.bfloat16)
        value = (wide * row(2)).astype(jnp.bfloat16)
        near = mask[...] != 0.0
        fresh = dot_nt(query, key)
        diag = unit_part * CHUNKS + ch
        expo = []
        for j in range(blocks):
            at = tiles(lax.rem(diag + j, blocks) * rows, rows)
            score = dot_nt(query, kvb[sec, 0, at])
            if j == 0:
                score = jnp.where(near, fresh, score)
            expo.append(jnp.exp2(score * (HD**-0.5 * math.log2(math.e)) - SHIFT))
        inverse = 1.0 / jnp.sum(sum(expo), axis=1, keepdims=True)
        mixed = None
        for j in range(blocks):
            at = tiles(lax.rem(diag + j, blocks) * rows, rows)
            weight = expo[j] * inverse
            if j == 0:
                mixed = dot_nn(jnp.where(near, weight, 0.0).astype(jnp.bfloat16), value)
                weight = jnp.where(near, 0.0, weight)
            mixed = mixed + dot_nn(weight.astype(jnp.bfloat16), kvb[sec, 1, at])
        return (wide + row(3) * mixed).astype(jnp.bfloat16)

    @pl.when(is_unit)
    def _():
        r = lax.broadcasted_iota(jnp.int32, (rows, rows), 0)
        t = lax.broadcasted_iota(jnp.int32, (rows, rows), 1)
        blk = tok // MB
        seen = (r // tok == t // tok) & (t // blk <= r // blk)
        mask[...] = jnp.where(seen, 1.0, 0.0)

        for ch in range(CHUNKS):
            pltpu.make_async_copy(xin.at[ch], xin.at[ch], xin_sem.at[ch]).wait()
            if ch == 0:
                pltpu.make_async_copy(gb.at[0], gb.at[0], g_sem.at[0]).wait()
                pltpu.make_async_copy(kvb.at[0], kvb.at[0], kv_sem.at[0]).wait()
            xmid[ch] = attend(ch, 0, xin[ch])
            if ch == 0:
                pltpu.make_async_copy(gb.at[1], gb.at[1], g_sem.at[1]).wait()
                pltpu.make_async_copy(kvb.at[1], kvb.at[1], kv_sem.at[1]).wait()
            xout[ch] = attend(ch, 1, xmid[ch])

            @pl.when(zh < last)
            def _():
                next_copy(ch).start()

            @pl.when(zh == last)
            def _():
                def fin_start(i, _):
                    for n in range(nd):
                        fin_copy(ch, i, n).start()
                    return 0

                lax.fori_loop(0, per_chunk, fin_start, 0)

            def ret_start(i, _):
                for sec in range(2):
                    ret_copy(ch, sec, i).start()
                return 0

            lax.fori_loop(0, per_chunk, ret_start, 0)

        for ch in range(CHUNKS):

            @pl.when(zh < last)
            def _():
                next_copy(ch).wait_send()

            @pl.when(zh == last)
            def _():
                def fin_wait(i, _):
                    for n in range(nd):
                        fin_copy(ch, i, n).wait_send()
                    return 0

                lax.fori_loop(0, per_chunk, fin_wait, 0)

            def ret_wait(i, _):
                for sec in range(2):
                    ret_copy(ch, sec, i).wait_send()
                return 0

            lax.fori_loop(0, per_chunk, ret_wait, 0)

    @pl.when(has_unit & (core == 1))
    def _():
        for i in range(4):
            g_copy(i).wait_send()

    def x_wait(i, _):
        x_copy(i).wait_send()
        return 0

    def kv_wait(i, _):
        mine, _, _, far = kv_copy(i)

        @pl.when(jnp.logical_not(mine))
        def _():
            far.wait_send()

        return 0

    @pl.when(s == 0)
    def _():
        lax.fori_loop(0, heads, x_wait, 0)

    lax.fori_loop(0, PARTS * heads, kv_wait, 0)
    pltpu.make_async_copy(fs_ref, fs_ref, fs_sem).wait()
    pltpu.make_async_copy(fin_ref.at[0], fin_ref.at[0], fin_sem.at[0]).wait()
    if slots == 2:

        @pl.when(h_last > h_first)
        def _():
            pltpu.make_async_copy(fin_ref.at[1], fin_ref.at[1], fin_sem.at[1]).wait()

        @pl.when(h_last == h_first)
        def _():
            fin_ref[1] = jnp.zeros(fin_ref.shape[1:], fin_ref.dtype)


def finish(dims, fs_ref, fin_ref, kg, vg, guided_ref, fresh_ref):
    heads, n_sec, n_patch, tok, width, nd, slots = dims
    out_w = width // (2 * n_sec)
    for h in range(heads):
        at = slice(h * HD, (h + 1) * HD)
        wide = fs_ref[:, at].astype(jnp.float32)
        normed = wide * lax.rsqrt(jnp.mean(wide * wide, axis=1, keepdims=True) + EPS)
        fresh_ref[0, :, at] = (normed * kg[:, at]).astype(jnp.bfloat16)
        fresh_ref[1, :, at] = (wide * vg[:, at]).astype(jnp.bfloat16)
    parts = []
    for slot in range(slots):
        uncond = fin_ref[slot, 0].astype(jnp.float32)
        cond = fin_ref[slot, 1].astype(jnp.float32)
        parts.append(uncond + guide_scale * (cond - uncond))
    both = jnp.concatenate(parts, axis=1) if slots == 2 else parts[0]
    col = lax.axis_index("cfg") * n_sec + lax.axis_index("section")
    off = lax.rem(out_w * col, HD)
    for start in sorted({(out_w * j) % HD for j in range(2 * n_sec)}):

        @pl.when(off == start)
        def _():
            guided_ref[...] = both[:, start : start + out_w].astype(jnp.bfloat16)


def local(dims, inputs, stale_kv, q_gain, k_gain, v_gain, o_gain):
    heads, n_sec, n_patch, tok, width, nd, slots = dims
    rows = n_patch * tok // (PARTS * CHUNKS)
    per_chunk = rows // tok
    dma = pltpu.SemaphoreType.DMA
    bf16 = jnp.bfloat16
    vmem = pl.BlockSpec(memory_space=pltpu.VMEM)
    far = pl.BlockSpec(memory_space=pl.ANY)
    fs, fin = pl.pallas_call(
        functools.partial(flow, dims),
        out_shape=(
            jax.ShapeDtypeStruct((tok, width), bf16),
            jax.ShapeDtypeStruct((slots, 2, tok, HD), bf16),
        ),
        in_specs=[far] * 6,
        out_specs=(vmem, vmem),
        scratch_shapes=[
            pltpu.VMEM((2, 2, n_patch * tok, HD), bf16),
            pltpu.VMEM((CHUNKS, rows, HD), bf16),
            pltpu.VMEM((CHUNKS, rows, HD), bf16),
            pltpu.VMEM((CHUNKS, rows, HD), bf16),
            pltpu.VMEM((2, 4, 1, HD), jnp.float32),
            pltpu.VMEM((rows, rows), jnp.float32),
            dma((PARTS * heads,)),
            dma((heads,)),
            dma((4,)),
            dma((CHUNKS,)),
            dma((CHUNKS, 2, per_chunk)),
            dma((CHUNKS, per_chunk, nd)),
            dma((2,)),
            dma((CHUNKS,)),
            dma((2,)),
            dma(()),
            dma((slots,)),
        ],
        compiler_params=pltpu.CompilerParams(collective_id=1, has_side_effects=True),
        name="flow",
    )(inputs[0], stale_kv[0, 0], q_gain, k_gain, v_gain, o_gain)
    guided, fresh = pl.pallas_call(
        functools.partial(finish, dims),
        out_shape=(
            jax.ShapeDtypeStruct((tok, width // (2 * n_sec)), bf16),
            jax.ShapeDtypeStruct((2, tok, width), bf16),
        ),
        in_specs=[vmem] * 4,
        out_specs=(vmem, vmem),
        name="finish",
    )(fs, fin, k_gain, v_gain)
    return guided, fresh[None, None]


def solution(mesh):
    n_cfg, n_sec, n_patch = mesh.shape["cfg"], mesh.shape["section"], mesh.shape["patch"]
    placed = (
        P("cfg", "patch", None),
        P("cfg", "section", None, "patch", None),
        P("section", None),
        P("section", None),
        P("section", None),
        P("section", None),
    )

    def whole(inputs, stale_kv, q_gain, k_gain, v_gain, o_gain):
        tok, width = inputs.shape[1] // n_patch, inputs.shape[2]
        heads = width // HD
        out_w = width // (n_cfg * n_sec)
        takers = {(HD * h + HD - 1) // out_w - (HD * h) // out_w + 1 for h in range(heads)}
        assert len(takers) == 1 and n_cfg == 2
        spans = [(out_w * j + out_w - 1) // HD - (out_w * j) // HD for j in range(n_cfg * n_sec)]
        dims = (heads, n_sec, n_patch, tok, width, takers.pop(), 1 + max(spans))
        return jax.shard_map(
            functools.partial(local, dims),
            mesh=mesh,
            in_specs=placed,
            out_specs=(P("patch", ("cfg", "section")), P("cfg", "section", None, "patch", None)),
            check_vma=False,
        )(inputs, stale_kv, q_gain, k_gain, v_gain, o_gain)

    return whole
```

time: 799 us -> 56.9 us (0.07)
  the two profiles are of different devices: /device:TPU:1 before, /device:TPU:179 now
where the time goes in v1:
time: 56.9 us; the launch traced here: 56.7 us
  Pallas kernels  56.1 us (99%)
  between operations  0.64 us (1%)
    pallas_call x1, Pallas kernels, local(): pl.pallas_call(functools.partial(flow, dims), out_shape=(jax.ShapeDtypeSt...  54.3 us
    pallas_call x1, Pallas kernels, local(): pl.pallas_call(functools.partial(finish, dims), out_shape=(jax.ShapeDtype...  1.81 us

profile of v1, /device:TPU:179, one launch (start us, length us, event | category | flops | bytes accessed | tf_op | source)
XLA Modules:
  0.0 56.7 jit_solution(6903969015421315253)
XLA Ops:
  0.6 54.3 %flow.1 = (bf16[32,1536]{1,0:T(8,128)(2,1)}, bf16[2,2,32,128]{3,2,1,0:T(8,128)(2,1)}) custom-call(bf16[32,1536]{1,0:T(8,128)(2,1)} %bitcast.4, bf16[2,32,1536]{2,1,0:T(8,128)(2,1)} %bitcast.3, f32[1,1536]{1,0:T(1,128)} %qg.1, f32[1,1536]{1,0:T(1,128)} %kg.3, f32[1,1536]{1,0:T(1,128)} %vg.3, f32[1,1536]{1,0:T(1,128)} %og.1), custom_call_target="tpu_custom_call" | custom-call | tf_op jit(solution)/shard_map/flow/pallas_call | solution.py:365
  54.9 1.8 %finish.1 = (bf16[32,96]{1,0:T(8,128)(2,1)}, bf16[2,32,1536]{2,1,0:T(8,128)(2,1)}) custom-call(bf16[32,1536]{1,0:T(8,128)(2,1)} %get-tuple-element.6.fs_ref, bf16[2,2,32,128]{3,2,1,0:T(8,128)(2,1)} %get-tuple-element.7.fin_ref, f32[1,1536]{1,0:T(1,128)} %kg.3, f32[1,1536]{1,0:T(1,128)} %vg.3), custom_call_target="tpu_custom_call" | custom-call | tf_op jit(solution)/shard_map/finish/pallas_call | solution.py:395

commit v2 on v1

v2 whole, which is shorter than its diff:
```python
import functools
import math

import jax
import jax.numpy as jnp
from jax import lax
from jax.experimental import pallas as pl
from jax.experimental.pallas import tpu as pltpu
from jax.sharding import PartitionSpec as P

MESH = pl.DeviceIdType.MESH
HD = 128
MB = 8
PARTS = 4
CHUNKS = 2
SHIFT = 24.0
EPS = 1e-6
guide_scale = 6.0


def dot_nt(a, b):
    return lax.dot_general(a, b, (((1,), (1,)), ((), ())), preferred_element_type=jnp.float32)


def dot_nn(a, b):
    return lax.dot_general(a, b, (((1,), (0,)), ((), ())), preferred_element_type=jnp.float32)


def tiles(start, size):
    return pl.ds(pl.multiple_of(start, size), size)


def flow(
    dims, x_ref, kv_ref, qg, kg, vg, og, fs_ref, fin_ref,
    kvb, xin, xmid, xout, gb, mask,
    kv_send, x_send, g_send, nxt_send, ret_send, fin_send,
    kv_sem, xin_sem, g_sem, fs_sem, fin_sem, rel_send, rel_sem, ret_ok, nxt_ok,
):
    heads, n_sec, n_patch, tok, width, nd, slots = dims
    quarter = n_patch // PARTS
    rows = xin.shape[1]
    per_chunk = rows // tok
    wide_keys = mask.shape[2]
    copies = wide_keys // rows
    blocks = n_patch * tok // wide_keys
    last = n_sec // 2 - 1
    out_w = width // (2 * n_sec)
    ny = 8 if n_patch == 32 else 2
    nx = n_patch // ny
    hy = ny // 2
    c, s, p = lax.axis_index("cfg"), lax.axis_index("section"), lax.axis_index("patch")
    zh = s // 2
    core = lax.rem(s, 2)
    s0 = zh * 2
    as_int = lambda flag: flag.astype(jnp.int32)

    def patch_at(pos):
        at = lax.rem(pos, 2 * quarter)
        return (at // hy) * ny + (pos // (2 * quarter)) * hy + lax.rem(at, hy)

    def owner(h, side, branch):
        at = lax.rem(h, hy)
        return lax.rem(at + branch + 1 + h // hy, nx) * ny + side * hy + at

    x, y = p // ny, lax.rem(p, ny)
    side, at_y = y // hy, lax.rem(y, hy)
    place = x * hy + at_y
    on_core = place // quarter
    place = lax.rem(place, quarter)
    nth = lax.rem(x - at_y - c - 1 + 2 * nx + hy * nx, nx)
    is_unit = nth < heads // hy
    head = lax.rem(nth * hy + at_y, heads)
    block_at = side * 2 + core
    col = c * n_sec + s
    h_first = (out_w * col) // HD
    h_last = (out_w * col + out_w - 1) // HD
    is_final = is_unit & (zh == last)
    gains = (qg, kg, vg, og)

    bar = pltpu.get_barrier_semaphore()
    other = s0 + 1 - core

    def hello(dev):
        pl.semaphore_signal(bar, inc=1, device_id=dev, device_id_type=MESH)

    def loop(n, body, first=0):
        def step(i, _):
            body(i)
            return 0

        lax.fori_loop(first, n, step, 0)

    @pl.when(is_unit)
    def _():
        def greet(i):
            q = lax.rem(p + i, n_patch)
            hello((c, s, q))

            @pl.when((lax.rem(q, ny) // hy == side) & (q // ny // (nx // 2) == core))
            def _():
                hello((c, other, q))

        hello((c, other, p))
        loop(n_patch, greet, 1)

        @pl.when(zh < last)
        def _():
            hello((c, s + 2, p))

        for i, g in enumerate(gains):
            pltpu.make_async_copy(g.at[:, tiles(head * HD, HD)], gb.at[core, i], g_sem.at[0]).start()

    for branch in range(2):
        for n in range(slots):
            h = (h_first, h_last)[n]
            wanted = jnp.logical_not(is_final & (on_core == core) & (c == branch) & (head == h))
            if n == 1:
                wanted = wanted & (h_last > h_first)

            @pl.when(wanted)
            def _():
                hello((branch, n_sec - 2 + on_core, owner(h, side, branch)))

    unit = as_int(is_unit)
    mine_too = is_final & (on_core == core) & (head >= h_first) & (head <= h_last)
    greeted = 2 * heads + as_int(on_core != core) * (heads - unit) + as_int(is_unit & (zh > 0))
    pl.semaphore_wait(bar, greeted + as_int(is_final) * (quarter * nd) - as_int(mine_too))

    def g_copy(i):
        return pltpu.make_async_remote_copy(
            src_ref=gains[i].at[:, tiles(head * HD, HD)],
            dst_ref=gb.at[core, i],
            send_sem=g_send.at[i],
            recv_sem=g_sem.at[1],
            device_id=(c, other, p),
            device_id_type=MESH,
        )

    def x_copy(i):
        h = lax.rem(p + i, heads)
        to = owner(h, side, c)
        src = x_ref.at[:, tiles(h * HD, HD)]
        dst = xin.at[place // per_chunk, tiles(lax.rem(place, per_chunk) * tok, tok)]
        far = pltpu.make_async_remote_copy(
            src_ref=src,
            dst_ref=dst,
            send_sem=x_send.at[i],
            recv_sem=xin_sem.at[place // per_chunk],
            device_id=(c, on_core, to),
            device_id_type=MESH,
        )
        return (to == p) & (on_core == 0), src, dst, xin_sem.at[place // per_chunk], far

    def kv_copy(i):
        k = lax.rem(p + i, 2 * heads)
        h = lax.rem(k, heads)
        to = owner(h, k // heads, c)
        at = (side * 2 + on_core) * quarter + place
        src = kv_ref.at[:, :, tiles(h * HD, HD)]
        dst = kvb.at[core, :, tiles(at * tok, tok)]
        sem = kv_sem.at[at * tok // wide_keys]
        far = pltpu.make_async_remote_copy(
            src_ref=src,
            dst_ref=dst,
            send_sem=kv_send.at[i],
            recv_sem=sem,
            device_id=(c, s, to),
            device_id_type=MESH,
        )
        return to == p, src, dst, sem, far

    def relay(i):
        block = kvb.at[core, :, slice(i * wide_keys, (i + 1) * wide_keys)]
        return pltpu.make_async_remote_copy(
            src_ref=block,
            dst_ref=block,
            send_sem=rel_send.at[i],
            recv_sem=rel_sem.at[i],
            device_id=(c, other, p),
            device_id_type=MESH,
        )

    def start(copy):
        mine, src, dst, sem, far = copy

        @pl.when(mine)
        def _():
            pltpu.make_async_copy(src, dst, sem).start()

        @pl.when(jnp.logical_not(mine))
        def _():
            far.start()

    def sent(copy):
        @pl.when(jnp.logical_not(copy[0]))
        def _():
            copy[4].wait_send()

    @pl.when(s == 0)
    def _():
        loop(heads, lambda i: start(x_copy(i)))

    loop(2 * heads, lambda i: start(kv_copy(i)))

    @pl.when(is_unit)
    def _():
        for i in range(4):
            g_copy(i).start()

    def ready(h):
        to = owner(h, side, c)

        @pl.when(jnp.logical_not((to == p) & (on_core == core)))
        def _():
            pl.semaphore_signal(ret_ok, inc=1, device_id=(c, s0 + on_core, to), device_id_type=MESH)

    loop(heads, ready)

    @pl.when(is_unit & (zh > 0))
    def _():
        pl.semaphore_signal(nxt_ok, inc=1, device_id=(c, s - 2, p), device_id_type=MESH)

    def next_copy(ch):
        return pltpu.make_async_remote_copy(
            src_ref=xout.at[ch],
            dst_ref=xin.at[ch],
            send_sem=nxt_send.at[ch],
            recv_sem=xin_sem.at[ch],
            device_id=(c, s + 2, p),
            device_id_type=MESH,
        )

    def ret_copy(ch, sec, i):
        to = patch_at(block_at * quarter + ch * per_chunk + i)
        src = (xin, xmid)[sec].at[ch, tiles(i * tok, tok)]
        dst = fs_ref.at[:, tiles(head * HD, HD)]
        far = pltpu.make_async_remote_copy(
            src_ref=src,
            dst_ref=dst,
            send_sem=ret_send.at[ch, sec, i],
            recv_sem=fs_sem,
            device_id=(c, s0 + sec, to),
            device_id_type=MESH,
        )
        return (to == p) & (core == sec), src, dst, fs_sem, far

    def fin_copy(ch, i, n):
        j = (HD * head) // out_w + n
        slot = head - (out_w * j) // HD
        to = patch_at(block_at * quarter + ch * per_chunk + i)
        src = xout.at[ch, tiles(i * tok, tok)]
        dst = fin_ref.at[slot, c]
        far = pltpu.make_async_remote_copy(
            src_ref=src,
            dst_ref=dst,
            send_sem=fin_send.at[ch, i, n],
            recv_sem=fin_sem.at[slot],
            device_id=(j // n_sec, lax.rem(j, n_sec), to),
            device_id_type=MESH,
        )
        return (to == p) & (j == col), src, dst, fin_sem.at[slot], far

    def attend(ch, sec, x):
        row = lambda i: gb[sec, i]
        wide = x.astype(jnp.float32)
        normed = wide * lax.rsqrt(jnp.mean(wide * wide, axis=1, keepdims=True) + EPS)
        query = (normed * row(0)).astype(jnp.bfloat16)
        key = (normed * row(1)).astype(jnp.bfloat16)
        value = (wide * row(2)).astype(jnp.bfloat16)
        near = mask[ch % copies] != 0.0
        fresh = dot_nt(query, jnp.concatenate([key] * copies, axis=0))
        diag = block_at * (CHUNKS // copies) + ch // copies
        expo = []
        for j in range(blocks):
            at = tiles(lax.rem(diag + j, blocks) * wide_keys, wide_keys)
            score = dot_nt(query, kvb[sec, 0, at])
            if j == 0:
                score = jnp.where(near, fresh, score)
            expo.append(jnp.exp2(score * (HD**-0.5 * math.log2(math.e)) - SHIFT))
        inverse = 1.0 / jnp.sum(sum(expo), axis=1, keepdims=True)
        mixed = None
        for j in range(blocks):
            at = tiles(lax.rem(diag + j, blocks) * wide_keys, wide_keys)
            weight = expo[j] * inverse
            if j == 0:
                mixed = dot_nn(
                    jnp.where(near, weight, 0.0).astype(jnp.bfloat16),
                    jnp.concatenate([value] * copies, axis=0),
                )
                weight = jnp.where(near, 0.0, weight)
            mixed = mixed + dot_nn(weight.astype(jnp.bfloat16), kvb[sec, 1, at])
        return (wide + row(3) * mixed).astype(jnp.bfloat16)

    @pl.when(is_unit)
    def _():
        blk = tok // MB
        for v in range(copies):
            r = lax.broadcasted_iota(jnp.int32, (rows, wide_keys), 0) + v * rows
            t = lax.broadcasted_iota(jnp.int32, (rows, wide_keys), 1)
            seen = (r // tok == t // tok) & (t // blk <= r // blk)
            mask[v] = jnp.where(seen, 1.0, 0.0)

        def relayed():
            for i in range(blocks):
                relay(i).wait_recv()

        for i in range(blocks):
            block = kvb.at[core, :, slice(i * wide_keys, (i + 1) * wide_keys)]
            pltpu.make_async_copy(block, block, kv_sem.at[i]).wait()
            relay(i).start()
        pltpu.make_async_copy(gb.at[0], gb.at[0], g_sem.at[0]).wait()
        pltpu.make_async_copy(gb.at[1], gb.at[1], g_sem.at[1]).wait()

        for ch in range(CHUNKS):
            pltpu.make_async_copy(xin.at[ch], xin.at[ch], xin_sem.at[ch]).wait()
            if ch == 0:
                pl.when(core == 1)(relayed)
            xmid[ch] = attend(ch, 0, xin[ch])
            if ch == 0:
                pl.when(core == 0)(relayed)
            xout[ch] = attend(ch, 1, xmid[ch])

            @pl.when(zh < last)
            def _():
                if ch == 0:
                    pl.semaphore_wait(nxt_ok, 1)
                next_copy(ch).start()

            @pl.when(zh == last)
            def _():
                def go(i):
                    for n in range(nd):
                        start(fin_copy(ch, i, n))

                loop(per_chunk, go)

            if ch == 0:
                pl.semaphore_wait(ret_ok, 2 * quarter - as_int(on_core == core))

            def go(i):
                for sec in range(2):
                    start(ret_copy(ch, sec, i))

            loop(per_chunk, go)

        for ch in range(CHUNKS):

            @pl.when(zh < last)
            def _():
                next_copy(ch).wait_send()

            @pl.when(zh == last)
            def _():
                def go(i):
                    for n in range(nd):
                        sent(fin_copy(ch, i, n))

                loop(per_chunk, go)

            def go(i):
                for sec in range(2):
                    sent(ret_copy(ch, sec, i))

            loop(per_chunk, go)

    @pl.when(is_unit)
    def _():
        for i in range(4):
            g_copy(i).wait_send()
        for i in range(blocks):
            relay(i).wait_send()

    @pl.when(s == 0)
    def _():
        loop(heads, lambda i: sent(x_copy(i)))

    loop(2 * heads, lambda i: sent(kv_copy(i)))
    pltpu.make_async_copy(fs_ref, fs_ref, fs_sem).wait()
    pltpu.make_async_copy(fin_ref.at[0], fin_ref.at[0], fin_sem.at[0]).wait()
    if slots == 2:

        @pl.when(h_last > h_first)
        def _():
            pltpu.make_async_copy(fin_ref.at[1], fin_ref.at[1], fin_sem.at[1]).wait()

        @pl.when(h_last == h_first)
        def _():
            fin_ref[1] = jnp.zeros(fin_ref.shape[1:], fin_ref.dtype)


def finish(dims, fs_ref, fin_ref, kg, vg, guided_ref, fresh_ref):
    heads, n_sec, n_patch, tok, width, nd, slots = dims
    out_w = width // (2 * n_sec)
    for h in range(heads):
        at = slice(h * HD, (h + 1) * HD)
        wide = fs_ref[:, at].astype(jnp.float32)
        normed = wide * lax.rsqrt(jnp.mean(wide * wide, axis=1, keepdims=True) + EPS)
        fresh_ref[0, :, at] = (normed * kg[:, at]).astype(jnp.bfloat16)
        fresh_ref[1, :, at] = (wide * vg[:, at]).astype(jnp.bfloat16)
    parts = []
    for slot in range(slots):
        uncond = fin_ref[slot, 0].astype(jnp.float32)
        cond = fin_ref[slot, 1].astype(jnp.float32)
        parts.append(uncond + guide_scale * (cond - uncond))
    both = jnp.concatenate(parts, axis=1) if slots == 2 else parts[0]
    col = lax.axis_index("cfg") * n_sec + lax.axis_index("section")
    off = lax.rem(out_w * col, HD)
    for start in sorted({(out_w * j) % HD for j in range(2 * n_sec)}):

        @pl.when(off == start)
        def _():
            guided_ref[...] = both[:, start : start + out_w].astype(jnp.bfloat16)


def local(dims, inputs, stale_kv, q_gain, k_gain, v_gain, o_gain):
    heads, n_sec, n_patch, tok, width, nd, slots = dims
    rows = n_patch * tok // (PARTS * CHUNKS)
    per_chunk = rows // tok
    wide_keys = min(256, n_patch * tok // PARTS)
    dma = pltpu.SemaphoreType.DMA
    bf16 = jnp.bfloat16
    vmem = pl.BlockSpec(memory_space=pltpu.VMEM)
    far = pl.BlockSpec(memory_space=pl.ANY)
    fs, fin = pl.pallas_call(
        functools.partial(flow, dims),
        out_shape=(
            jax.ShapeDtypeStruct((tok, width), bf16),
            jax.ShapeDtypeStruct((slots, 2, tok, HD), bf16),
        ),
        in_specs=[far] * 6,
        out_specs=(vmem, vmem),
        scratch_shapes=[
            pltpu.VMEM((2, 2, n_patch * tok, HD), bf16),
            pltpu.VMEM((CHUNKS, rows, HD), bf16),
            pltpu.VMEM((CHUNKS, rows, HD), bf16),
            pltpu.VMEM((CHUNKS, rows, HD), bf16),
            pltpu.VMEM((2, 4, 1, HD), jnp.float32),
            pltpu.VMEM((wide_keys // rows, rows, wide_keys), jnp.float32),
            dma((2 * heads,)),
            dma((heads,)),
            dma((4,)),
            dma((CHUNKS,)),
            dma((CHUNKS, 2, per_chunk)),
            dma((CHUNKS, per_chunk, nd)),
            dma((n_patch * tok // wide_keys,)),
            dma((CHUNKS,)),
            dma((2,)),
            dma(()),
            dma((slots,)),
            dma((n_patch * tok // wide_keys,)),
            dma((n_patch * tok // wide_keys,)),
            pltpu.SemaphoreType.REGULAR,
            pltpu.SemaphoreType.REGULAR,
        ],
        compiler_params=pltpu.CompilerParams(collective_id=1, has_side_effects=True),
        name="flow",
    )(inputs[0], stale_kv[0, 0], q_gain, k_gain, v_gain, o_gain)
    guided, fresh = pl.pallas_call(
        functools.partial(finish, dims),
        out_shape=(
            jax.ShapeDtypeStruct((tok, width // (2 * n_sec)), bf16),
            jax.ShapeDtypeStruct((2, tok, width), bf16),
        ),
        in_specs=[vmem] * 4,
        out_specs=(vmem, vmem),
        name="finish",
    )(fs, fin, k_gain, v_gain)
    return guided, fresh[None, None]


def solution(mesh):
    n_cfg, n_sec, n_patch = mesh.shape["cfg"], mesh.shape["section"], mesh.shape["patch"]
    placed = (
        P("cfg", "patch", None),
        P("cfg", "section", None, "patch", None),
        P("section", None),
        P("section", None),
        P("section", None),
        P("section", None),
    )

    def whole(inputs, stale_kv, q_gain, k_gain, v_gain, o_gain):
        tok, width = inputs.shape[1] // n_patch, inputs.shape[2]
        heads = width // HD
        out_w = width // (n_cfg * n_sec)
        takers = {(HD * h + HD - 1) // out_w - (HD * h) // out_w + 1 for h in range(heads)}
        assert len(takers) == 1 and n_cfg == 2
        spans = [(out_w * j + out_w - 1) // HD - (out_w * j) // HD for j in range(n_cfg * n_sec)]
        dims = (heads, n_sec, n_patch, tok, width, takers.pop(), 1 + max(spans))
        return jax.shard_map(
            functools.partial(local, dims),
            mesh=mesh,
            in_specs=placed,
            out_specs=(P("patch", ("cfg", "section")), P("cfg", "section", None, "patch", None)),
            check_vma=False,
        )(inputs, stale_kv, q_gain, k_gain, v_gain, o_gain)

    return whole
```

time: 56.9 us -> 50.2 us (0.88)
  the two profiles are of different devices: /device:TPU:179 before, /device:TPU:1 now
where the time goes in v2:
time: 50.2 us; the launch traced here: 50.1 us
  Pallas kernels  49.4 us (98%)
  between operations  0.64 us (1%)
    pallas_call x1, Pallas kernels, local(): pl.pallas_call(functools.partial(flow, dims), out_shape=(jax.ShapeDtypeSt...  47.6 us
    pallas_call x1, Pallas kernels, local(): pl.pallas_call(functools.partial(finish, dims), out_shape=(jax.ShapeDtype...  1.82 us

profile of v2, /device:TPU:1, one launch (start us, length us, event | category | flops | bytes accessed | tf_op | source)
XLA Modules:
  0.0 50.1 jit_solution(17242498715303575998)
XLA Ops:
  0.6 47.6 %flow.1 = (bf16[32,1536]{1,0:T(8,128)(2,1)}, bf16[2,2,32,128]{3,2,1,0:T(8,128)(2,1)}) custom-call(bf16[32,1536]{1,0:T(8,128)(2,1)} %bitcast.4, bf16[2,32,1536]{2,1,0:T(8,128)(2,1)} %bitcast.3, f32[1,1536]{1,0:T(1,128)} %qg.1, f32[1,1536]{1,0:T(1,128)} %kg.3, f32[1,1536]{1,0:T(1,128)} %vg.3, f32[1,1536]{1,0:T(1,128)} %og.1), custom_call_target="tpu_custom_call" | custom-call | tf_op jit(solution)/shard_map/flow/pallas_call | solution.py:424
  48.2 1.8 %finish.1 = (bf16[32,96]{1,0:T(8,128)(2,1)}, bf16[2,32,1536]{2,1,0:T(8,128)(2,1)}) custom-call(bf16[32,1536]{1,0:T(8,128)(2,1)} %get-tuple-element.6.fs_ref, bf16[2,2,32,128]{3,2,1,0:T(8,128)(2,1)} %get-tuple-element.7.fin_ref, f32[1,1536]{1,0:T(1,128)} %kg.3, f32[1,1536]{1,0:T(1,128)} %vg.3), custom_call_target="tpu_custom_call" | custom-call | tf_op jit(solution)/shard_map/finish/pallas_call | solution.py:458

commit v3 on v2

--- a/solution.py
+++ b/solution.py
@@ -28,6 +28,12 @@
 
 def tiles(start, size):
     return pl.ds(pl.multiple_of(start, size), size)
+
+
+def swapped(whole, at, piece):
+    parts = [whole[:, : at.start], piece, whole[:, at.stop :]]
+    parts = [part for part in parts if part.shape[1]]
+    return jnp.concatenate(parts, axis=1) if len(parts) > 1 else piece
 
 
 def flow(
@@ -40,7 +46,7 @@
     quarter = n_patch // PARTS
     rows = xin.shape[1]
     per_chunk = rows // tok
-    wide_keys = mask.shape[2]
+    wide_keys = min(256, n_patch * tok // PARTS)
     copies = wide_keys // rows
     blocks = n_patch * tok // wide_keys
     last = n_sec // 2 - 1
@@ -152,9 +158,12 @@
         return (to == p) & (on_core == 0), src, dst, xin_sem.at[place // per_chunk], far
 
     def kv_copy(i):
-        k = lax.rem(p + i, 2 * heads)
-        h = lax.rem(k, heads)
-        to = owner(h, k // heads, c)
+        k = lax.rem(p + i, 8)
+        h = i // 8 * 2 + lax.rem(k, 2) + lax.rem(k // 2, 2) * (heads // 2)
+        to_side = k // 4
+        if heads % 6:
+            h, to_side = lax.rem(i, heads), i // heads
+        to = owner(h, to_side, c)
         at = (side * 2 + on_core) * quarter + place
         src = kv_ref.at[:, :, tiles(h * HD, HD)]
         dst = kvb.at[core, :, tiles(at * tok, tok)]
@@ -267,15 +276,16 @@
         query = (normed * row(0)).astype(jnp.bfloat16)
         key = (normed * row(1)).astype(jnp.bfloat16)
         value = (wide * row(2)).astype(jnp.bfloat16)
-        near = mask[ch % copies] != 0.0
-        fresh = dot_nt(query, jnp.concatenate([key] * copies, axis=0))
+        near = mask[...] != 0.0
+        fresh = dot_nt(query, key)
+        own = slice(ch % copies * rows, (ch % copies + 1) * rows)
         diag = block_at * (CHUNKS // copies) + ch // copies
         expo = []
         for j in range(blocks):
             at = tiles(lax.rem(diag + j, blocks) * wide_keys, wide_keys)
             score = dot_nt(query, kvb[sec, 0, at])
             if j == 0:
-                score = jnp.where(near, fresh, score)
+                score = swapped(score, own, jnp.where(near, fresh, score[:, own]))
             expo.append(jnp.exp2(score * (HD**-0.5 * math.log2(math.e)) - SHIFT))
         inverse = 1.0 / jnp.sum(sum(expo), axis=1, keepdims=True)
         mixed = None
@@ -283,22 +293,18 @@
             at = tiles(lax.rem(diag + j, blocks) * wide_keys, wide_keys)
             weight = expo[j] * inverse
             if j == 0:
-                mixed = dot_nn(
-                    jnp.where(near, weight, 0.0).astype(jnp.bfloat16),
-                    jnp.concatenate([value] * copies, axis=0),
-                )
-                weight = jnp.where(near, 0.0, weight)
+                mixed = dot_nn(jnp.where(near, weight[:, own], 0.0).astype(jnp.bfloat16), value)
+                weight = swapped(weight, own, jnp.where(near, 0.0, weight[:, own]))
             mixed = mixed + dot_nn(weight.astype(jnp.bfloat16), kvb[sec, 1, at])
         return (wide + row(3) * mixed).astype(jnp.bfloat16)
 
     @pl.when(is_unit)
     def _():
         blk = tok // MB
-        for v in range(copies):
-            r = lax.broadcasted_iota(jnp.int32, (rows, wide_keys), 0) + v * rows
-            t = lax.broadcasted_iota(jnp.int32, (rows, wide_keys), 1)
-            seen = (r // tok == t // tok) & (t // blk <= r // blk)
-            mask[v] = jnp.where(seen, 1.0, 0.0)
+        r = lax.broadcasted_iota(jnp.int32, (rows, rows), 0)
+        t = lax.broadcasted_iota(jnp.int32, (rows, rows), 1)
+        seen = (r // tok == t // tok) & (t // blk <= r // blk)
+        mask[...] = jnp.where(seen, 1.0, 0.0)
 
         def relayed():
             for i in range(blocks):
@@ -382,10 +388,6 @@
         @pl.when(h_last > h_first)
         def _():
             pltpu.make_async_copy(fin_ref.at[1], fin_ref.at[1], fin_sem.at[1]).wait()
-
-        @pl.when(h_last == h_first)
-        def _():
-            fin_ref[1] = jnp.zeros(fin_ref.shape[1:], fin_ref.dtype)
 
 
 def finish(dims, fs_ref, fin_ref, kg, vg, guided_ref, fresh_ref):
@@ -428,14 +430,14 @@
             jax.ShapeDtypeStruct((slots, 2, tok, HD), bf16),
         ),
         in_specs=[far] * 6,
-        out_specs=(vmem, vmem),
+        out_specs=(far, far),
         scratch_shapes=[
             pltpu.VMEM((2, 2, n_patch * tok, HD), bf16),
             pltpu.VMEM((CHUNKS, rows, HD), bf16),
             pltpu.VMEM((CHUNKS, rows, HD), bf16),
             pltpu.VMEM((CHUNKS, rows, HD), bf16),
             pltpu.VMEM((2, 4, 1, HD), jnp.float32),
-            pltpu.VMEM((wide_keys // rows, rows, wide_keys), jnp.float32),
+            pltpu.VMEM((rows, rows), jnp.float32),
             dma((2 * heads,)),
             dma((heads,)),
             dma((4,)),

time: 50.2 us -> 48.1 us (0.958)
  the two profiles are of different devices: /device:TPU:1 before, /device:TPU:63 now
where the time goes in v3:
time: 48.1 us; the launch traced here: 47.9 us
  Pallas kernels  47.3 us (98%)
  between operations  0.64 us (1%)
    pallas_call x1, Pallas kernels, local(): pl.pallas_call(functools.partial(flow, dims), out_shape=(jax.ShapeDtypeSt...  45.5 us
    pallas_call x1, Pallas kernels, local(): pl.pallas_call(functools.partial(finish, dims), out_shape=(jax.ShapeDtype...  1.82 us

profile of v3, /device:TPU:63, one launch (start us, length us, event | category | flops | bytes accessed | tf_op | source)
XLA Modules:
  0.0 47.9 jit_solution(3461631384048131298)
XLA Ops:
  0.6 45.5 %flow.1 = (bf16[32,1536]{1,0:T(8,128)(2,1)}, bf16[2,2,32,128]{3,2,1,0:T(8,128)(2,1)}) custom-call(bf16[32,1536]{1,0:T(8,128)(2,1)} %bitcast.4, bf16[2,32,1536]{2,1,0:T(8,128)(2,1)} %bitcast.3, f32[1,1536]{1,0:T(1,128)} %qg.1, f32[1,1536]{1,0:T(1,128)} %kg.3, f32[1,1536]{1,0:T(1,128)} %vg.3, f32[1,1536]{1,0:T(1,128)} %og.1), custom_call_target="tpu_custom_call" | custom-call | tf_op jit(solution)/shard_map/flow/pallas_call | solution.py:426
  46.1 1.8 %finish.1 = (bf16[32,96]{1,0:T(8,128)(2,1)}, bf16[2,32,1536]{2,1,0:T(8,128)(2,1)}) custom-call(bf16[32,1536]{1,0:T(8,128)(2,1)} %get-tuple-element.6.fs_ref, bf16[2,2,32,128]{3,2,1,0:T(8,128)(2,1)} %get-tuple-element.7.fin_ref, f32[1,1536]{1,0:T(1,128)} %kg.3, f32[1,1536]{1,0:T(1,128)} %vg.3), custom_call_target="tpu_custom_call" | custom-call | tf_op jit(solution)/shard_map/finish/pallas_call | solution.py:460

commit v4 on v3

--- a/solution.py
+++ b/solution.py
@@ -98,16 +98,16 @@
 
     @pl.when(is_unit)
     def _():
-        def greet(i):
-            q = lax.rem(p + i, n_patch)
-            hello((c, s, q))
-
-            @pl.when((lax.rem(q, ny) // hy == side) & (q // ny // (nx // 2) == core))
+        def greet_other(i):
+            q = patch_at(block_at * quarter + i)
+
+            @pl.when(q != p)
             def _():
                 hello((c, other, q))
 
+        loop(n_patch, lambda i: hello((c, s, lax.rem(p + i, n_patch))), 1)
+        loop(quarter, greet_other)
         hello((c, other, p))
-        loop(n_patch, greet, 1)
 
         @pl.when(zh < last)
         def _():
@@ -205,11 +205,14 @@
         def _():
             copy[4].wait_send()
 
+    first_kv = min(8, 2 * heads)
+    loop(first_kv, lambda i: start(kv_copy(i)))
+
     @pl.when(s == 0)
     def _():
         loop(heads, lambda i: start(x_copy(i)))
 
-    loop(2 * heads, lambda i: start(kv_copy(i)))
+    loop(2 * heads, lambda i: start(kv_copy(i)), first_kv)
 
     @pl.when(is_unit)
     def _():
@@ -340,8 +343,8 @@
 
                 loop(per_chunk, go)
 
-            if ch == 0:
-                pl.semaphore_wait(ret_ok, 2 * quarter - as_int(on_core == core))
+        pl.semaphore_wait(ret_ok, 2 * quarter - as_int(on_core == core))
+        for ch in range(CHUNKS):
 
             def go(i):
                 for sec in range(2):

time: 48.1 us -> 45.6 us (0.948)
  the two profiles are of different devices: /device:TPU:63 before, /device:TPU:1 now
where the time goes in v4:
time: 45.6 us; the launch traced here: 45.1 us
  Pallas kernels  44.5 us (98%)
  between operations  0.64 us (1%)
    pallas_call x1, Pallas kernels, local(): pl.pallas_call(functools.partial(flow, dims), out_shape=(jax.ShapeDtypeSt...  42.6 us
    pallas_call x1, Pallas kernels, local(): pl.pallas_call(functools.partial(finish, dims), out_shape=(jax.ShapeDtype...  1.82 us

profile of v4, /device:TPU:1, one launch (start us, length us, event | category | flops | bytes accessed | tf_op | source)
XLA Modules:
  0.0 45.1 jit_solution(1520071876503041881)
XLA Ops:
  0.6 42.6 %flow.1 = (bf16[32,1536]{1,0:T(8,128)(2,1)}, bf16[2,2,32,128]{3,2,1,0:T(8,128)(2,1)}) custom-call(bf16[32,1536]{1,0:T(8,128)(2,1)} %bitcast.4, bf16[2,32,1536]{2,1,0:T(8,128)(2,1)} %bitcast.3, f32[1,1536]{1,0:T(1,128)} %qg.1, f32[1,1536]{1,0:T(1,128)} %kg.3, f32[1,1536]{1,0:T(1,128)} %vg.3, f32[1,1536]{1,0:T(1,128)} %og.1), custom_call_target="tpu_custom_call" | custom-call | tf_op jit(solution)/shard_map/flow/pallas_call | solution.py:429
  43.3 1.8 %finish.1 = (bf16[32,96]{1,0:T(8,128)(2,1)}, bf16[2,32,1536]{2,1,0:T(8,128)(2,1)}) custom-call(bf16[32,1536]{1,0:T(8,128)(2,1)} %get-tuple-element.6.fs_ref, bf16[2,2,32,128]{3,2,1,0:T(8,128)(2,1)} %get-tuple-element.7.fin_ref, f32[1,1536]{1,0:T(1,128)} %kg.3, f32[1,1536]{1,0:T(1,128)} %vg.3), custom_call_target="tpu_custom_call" | custom-call | tf_op jit(solution)/shard_map/finish/pallas_call | solution.py:463
